TPU v7x, 1024 devices: a whole 4x8x16 slice. The times are simulated.
1024 devices in a mesh: grp: 32 (over z, core), mem: 32 (over y, x).
Axes of the slice: x: 4, y: 8, z: 16, core: 2. Of those that a mesh axis runs over, the one named last changes fastest.
Arguments:
- t_store: bfloat16 [16384, 4, 4096], P(('grp', 'mem')), may hold values from -6 to 6
- v_blocks: bfloat16 [11264, 32, 4096], P(('grp', 'mem')), may hold values from -0.0048828125 to 0.0048828125
- block_id: int32 [32, 32], P('grp'), may hold values from 0 to 31, each once within a row
- tile_home: int32 [32, 512], P('grp'), may hold values from 0 to 511, as said below
- task_slab: int32 [32, 32, 11], P('grp'), may hold values from 0 to 31, as said below
Outputs:
- ladder: float32 [64, 1024], P('grp', 'mem')
Inputs may be any that keep to these rules, and one draw needn't show every extreme that they name: `block_id`: each row is a permutation: every cd tile pair of a group is taken by exactly one mem device of it. tile_home[g, q*16+o] = m*16+s places occupied block o of cd tile pair q of group g in slot s of mem device m of that group; each row is a permutation; the tiles of one cd tile pair lie on cyclically consecutive mem devices, tile o on the device after that of tile o-1, so each mem device holds at most 1 tiles of every cd tile pair. The 11 entries of task_slab[g, d] are distinct ab slabs; slabs k*1 to k + 1 - 1 are the slabs of mem device k, and every device's entries include all 1 slabs of at least one mem device.
All inputs are finite; a program needn't handle non-finite values.
Results may differ from a plain program's by a relative error of at most 0.0003.
Values may be sent and summed in bfloat16 or wider, within the bound.
A program may use at most 32 MiB of HBM per device.

v0:
```python
import jax
import jax.numpy as jnp
from jax import lax
from jax.sharding import PartitionSpec as P

SLABS = 32


def rank_items(owner_rows):
    item_count = owner_rows.shape[1]
    positions = jnp.arange(item_count, dtype=jnp.int32)
    earlier = positions[:, None] > positions[None, :]
    same_owner = owner_rows[:, :, None] == owner_rows[:, None, :]
    return jnp.sum(same_owner & earlier[None], axis=2)


def pack_tiles(flat_store, owner_rows, slot_rows, rank_rows, own_index, capacity):
    at_owner = owner_rows == own_index
    seats = jnp.arange(capacity, dtype=jnp.int32)
    matches = at_owner[:, :, None] & (rank_rows[:, :, None] == seats[None, None, :])
    chosen = jnp.sum(jnp.where(matches, slot_rows[:, :, None], 0), axis=1)
    filled = jnp.any(matches, axis=1)
    picked = jnp.take(flat_store, chosen, axis=0)
    return jnp.where(filled[:, :, None], picked, jnp.zeros((), flat_store.dtype))


def body(t_store, v_blocks, block_id, tile_home, task_slab):
    members = lax.axis_size("mem")
    own_index = lax.axis_index("mem")
    occ_blocks = t_store.shape[0]
    tile_rows = t_store.shape[1]
    pair_width = t_store.shape[2]
    slab_width = v_blocks.shape[1]
    slab_mem = SLABS // members
    occ_rows = occ_blocks * tile_rows
    pair_all = block_id[0]
    tile_keys = pair_all[:, None] * occ_blocks + jnp.arange(occ_blocks, dtype=jnp.int32)[None, :]
    places = jnp.take(tile_home[0], tile_keys, axis=0)
    owners = places // occ_blocks
    slot_index = places % occ_blocks
    per_owner = (occ_blocks + members - 1) // members
    rank_index = rank_items(owners)
    flat_store = t_store.reshape(occ_blocks, tile_rows * pair_width)
    outgoing = pack_tiles(flat_store, owners, slot_index, rank_index, own_index, per_owner)
    row_index = owners[own_index] * per_owner + rank_index[own_index]
    incoming = lax.all_to_all(outgoing, "mem", split_axis=0, concat_axis=0, tiled=True)
    flat_in = incoming.reshape(members * per_owner, tile_rows * pair_width)
    fetched = jnp.take(flat_in, row_index, axis=0).reshape(occ_rows, pair_width)
    products = jnp.einsum("rk,bnk->rbn", fetched, v_blocks, preferred_element_type=jnp.float32)
    my_slabs = task_slab[0][own_index]
    one_hot = (my_slabs[:, None] == jnp.arange(SLABS, dtype=jnp.int32)[None, :]).astype(jnp.float32)
    dense_part = jnp.einsum("rbn,bs->rsn", products, one_hot, precision=lax.Precision.HIGHEST)
    dense_part = dense_part.reshape(occ_rows, SLABS * slab_width)
    received = lax.all_to_all(dense_part, "mem", split_axis=1, concat_axis=1, tiled=True)
    owned = jnp.sum(received.reshape(occ_rows, members, slab_mem * slab_width), axis=1)
    return lax.psum_scatter(owned, "grp", scatter_dimension=0, tiled=True)


def solution(mesh):
    return jax.shard_map(
        body,
        mesh=mesh,
        in_specs=(
            P(("grp", "mem"), None, None),
            P(("grp", "mem"), None, None),
            P("grp", None),
            P("grp", None),
            P("grp", None, None),
        ),
        out_specs=P("grp", "mem"),
        check_vma=False,
    )
```

profile of v0, /device:TPU:1, one launch (start us, length us, event | category | flops | bytes accessed | tf_op | source)
XLA Modules:
  0.0 196.3 jit_solution(15829700851913889414)
XLA Ops:
  0.0 0.8 multiply_bitcast_fusion
  0.9 0.1 reshape.312
  1.0 3.5 %gather_fusion = s32[512]{0:T(512)S(1)} fusion(s32[512]{0:T(512)S(1)} %bitcast.37, s32[1024]{0:T(1024)S(1)} %pad_clamp_fusion.2), kind=kCustom, calls=%fused_computation | custom fusion | bytes 6144 | tf_op jit(solution)/shard_map/jit(_take)/gather | solution.py:38
  4.7 0.1 convert_reduce_fusion
  4.9 1.3 copy.30
  6.2 2.2 %gather_fusion.1 = bf16[32,16384]{1,0:T(8,128)(2,1)} fusion(bf16[16,16384]{1,0:T(8,128)(2,1)S(1)} %bitcast.38, s32[1024]{0:T(1024)S(1)} %pad_clamp_fusion.1), kind=kCustom, calls=%fused_computation.1 | custom fusion | bytes 2097280 | tf_op jit(solution)/shard_map/jit(_take)/gather | solution.py:23
  8.5 2.4 %fusion = bf16[32,1,16384]{2,0,1:T(8,128)(2,1)} fusion(bf16[32,16384]{1,0:T(8,128)(2,1)} %gather_fusion.1, pred[32]{0:T(512)(128)(4,1)S(1)} %compare_and_fusion.1, pred[32]{0:T(512)(128)(4,1)S(1)} %get-tuple-element.5), kind=kLoop, calls=%fused_computation.6 | loop fusion | flops 1048576 | bytes 2097216 | tf_op jit(solution)/shard_map/jit(_where)/select_n | solution.py:24
  10.9 0.5 broadcast.400
  11.4 3.3 %reduce.8 = bf16[32,16384]{1,0:T(8,128)(2,1)} reduce(bf16[32,1,16384]{2,0,1:T(8,128)(2,1)} %fusion, bf16[]{:T(256)} %broadcast.400), dimensions={1}, to_apply=%copy.23.reduce_sub_computation | reduce | bytes 2097154 | tf_op jit(solution)/shard_map/jit(_where)/select_n | solution.py:24
  14.8 2.6 %reshape.341 = bf16[32,2,8192]{2,1,0:T(2,128)(2,1)} reshape(bf16[32,16384]{1,0:T(8,128)(2,1)} %reduce.8) | data formatting | bytes 2097152
  17.4 10.6 %all-to-all-start = ((bf16[32,2,8192]{2,1,0:T(2,128)(2,1)}), bf16[32,2,8192]{2,1,0:T(2,128)(2,1)}, u32[]{:S(2)}, u32[]{:S(2)}) async-start(bf16[32,2,8192]{2,1,0:T(2,128)(2,1)} %reshape.341), calls=%async_computation | async-start | bytes 2097152 | tf_op jit(solution)/shard_map/all_to_all | solution.py:46
  28.1 0.2 add_reduce_fusion
  28.3 0.1 broadcast_in_dim.57
  28.5 0.4 dynamic-slice_reduce_fusion
  28.9 18.2 %all-to-all-done = bf16[32,2,8192]{2,1,0:T(2,128)(2,1)} async-done(((bf16[32,2,8192]{2,1,0:T(2,128)(2,1)}), bf16[32,2,8192]{2,1,0:T(2,128)(2,1)}, u32[]{:S(2)}, u32[]{:S(2)}) %all-to-all-start) | async-done | bytes 1048608 | tf_op jit(solution)/shard_map/all_to_all | solution.py:46
  47.0 5.8 %reshape.342 = bf16[32,1,16384]{2,1,0:T(2,128)(2,1)} reshape(bf16[32,2,8192]{2,1,0:T(2,128)(2,1)} %all-to-all-done) | data formatting | bytes 2097152
  52.8 3.7 %copy.35 = bf16[32,1,16384]{2,0,1:T(8,128)(2,1)} copy(bf16[32,1,16384]{2,1,0:T(2,128)(2,1)} %reshape.342) | data formatting | bytes 2097152
  56.5 2.7 %gather_fusion.2 = bf16[16,16384]{1,0:T(8,128)(2,1)S(1)} fusion(bf16[32,16384]{1,0:T(8,128)(2,1)} %bitcast.39, s32[1024]{0:T(1024)S(1)} %pad_clamp_fusion), kind=kCustom, calls=%fused_computation.2 | custom fusion | bytes 1048640 | tf_op jit(solution)/shard_map/jit(_take)/gather | solution.py:48
  59.2 1.2 gather.17
  60.4 2.0 %fusion.1 = f32[64,11,32]{0,2,1:T(8,128)S(1)} fusion(bf16[11,32,4096]{2,1,0:T(8,128)(2,1)S(1)} %copy-done, bf16[64,4096]{1,0:T(8,128)(2,1)} %gather.17, pred[64]{0:T(512)(128)(4,1)S(1)} %broadcast_in_dim.57), kind=kOutput, calls=%fused_computation.7 | convolution fusion | flops 184811520 | bytes 3498048 | tf_op jit(solution)/shard_map/rk,bnk->rbn/dot_general | solution.py:49
  62.4 0.5 convolution_bitcast_fusion
  62.9 0.3 copy.36
  63.2 1.0 reshape.343
  64.3 6.8 %all-to-all-start.1 = ((f32[32,1,2048]{2,1,0:T(1,128)}), f32[32,1,2048]{2,1,0:T(1,128)S(1)}, u32[]{:S(2)}, u32[]{:S(2)}) async-start(f32[32,1,2048]{2,1,0:T(1,128)} %reshape.343), calls=%async_computation.1 | async-start | bytes 524288 | tf_op jit(solution)/shard_map/all_to_all | solution.py:54
  71.1 1.3 dynamic-slice.1
  73.0 8.5 %all-to-all-done.1 = f32[32,1,2048]{2,1,0:T(1,128)S(1)} async-done(((f32[32,1,2048]{2,1,0:T(1,128)}), f32[32,1,2048]{2,1,0:T(1,128)S(1)}, u32[]{:S(2)}, u32[]{:S(2)}) %all-to-all-start.1) | async-done | bytes 262176 | tf_op jit(solution)/shard_map/all_to_all | solution.py:54
  81.5 0.5 broadcast.401
  82.0 2.0 %reduce.9 = f32[32,2048]{1,0:T(8,128)} reduce(f32[32,1,2048]{2,1,0:T(1,128)S(1)} %all-to-all-done.1, f32[]{:T(128)} %broadcast.401), dimensions={1}, to_apply=%all_to_all.8.reduce_sub_computation | reduce | bytes 524292 | tf_op jit(solution)/shard_map/all_to_all | solution.py:54
  84.0 1.1 reshape.344
  85.2 0.1 copy.27
  85.2 110.5 %all-reduce = f32[64,32]{1,0:T(8,128)S(1)} all-reduce(f32[64,32]{1,0:T(8,128)S(1)} %copy.27), channel_id=2, replica_groups=mesh['grp'=32,'mem'=32] {'grp'}, use_global_device_ids=true, to_apply=%region_4.5.clone | all-reduce | flops 2048 | bytes 16384
  195.7 0.6 constant_dynamic-slice_fusion
  (22 shorter events, 0.5 us)
Async XLA Ops:
  0.0 60.4 %copy-start = (bf16[11,32,4096]{2,1,0:T(8,128)(2,1)S(1)}, bf16[11,32,4096]{2,1,0:T(8,128)(2,1)}, u32[]{:S(2)}) copy-start(bf16[11,32,4096]{2,1,0:T(8,128)(2,1)} %param.6) | copy-start | bytes 8650756
  0.0 1.0 copy-start.1
  11.4 17.0 %copy-start.2 = (s32[1,32,11]{1,0,2:T(1,128)S(1)}, s32[1,32,11]{1,0,2:T(1,128)}, u32[]{:S(2)}) copy-start(s32[1,32,11]{1,0,2:T(1,128)} %param.9) | copy-start | bytes 4228
  17.4 29.6 %all-to-all-start = ((bf16[32,2,8192]{2,1,0:T(2,128)(2,1)}), bf16[32,2,8192]{2,1,0:T(2,128)(2,1)}, u32[]{:S(2)}, u32[]{:S(2)}) async-start(bf16[32,2,8192]{2,1,0:T(2,128)(2,1)} %reshape.341), calls=%async_computation | async-start | bytes 2097152 | tf_op jit(solution)/shard_map/all_to_all | solution.py:46
  64.3 17.2 %all-to-all-start.1 = ((f32[32,1,2048]{2,1,0:T(1,128)}), f32[32,1,2048]{2,1,0:T(1,128)S(1)}, u32[]{:S(2)}, u32[]{:S(2)}) async-start(f32[32,1,2048]{2,1,0:T(1,128)} %reshape.343), calls=%async_computation.1 | async-start | bytes 524288 | tf_op jit(solution)/shard_map/all_to_all | solution.py:54
where the time goes:
time: 198 us; the launch traced here: 196 us
  blocking collectives  111 us (56%)
  local copies, waits for them, and re-layouts  29.3 us (15%)
  waiting for transfers between devices  26.6 us (13%)
  starting transfers between devices  17.4 us (9%)
  other arithmetic  9.14 us (5%)
  matrix products  2.49 us (1%)
    unnamed x1, blocking collectives  111 us
    all_to_all x1, waiting for transfers between devices, body(): lax.all_to_all(outgoing, 'mem', split_axis=0, concat_axis=0, tiled=True)  18.2 us
    unnamed x14, local copies, waits for them, and re-layouts  17.5 us
    all_to_all x1, starting transfers between devices, body(): lax.all_to_all(outgoing, 'mem', split_axis=0, concat_axis=0, tiled=True)  10.6 us
    all_to_all x1, waiting for transfers between devices, body(): lax.all_to_all(dense_part, 'mem', split_axis=1, concat_axis=1, tiled=True)  8.47 us
    all_to_all x1, starting transfers between devices, body(): lax.all_to_all(dense_part, 'mem', split_axis=1, concat_axis=1, tiled=True)  6.8 us
    select_n x2, other arithmetic, pack_tiles(): jnp.where(filled[:, :, None], picked, jnp.zeros((), flat_store.dtype))  5.79 us
  transfers between devices with their start and end apart: 2, of which 2 were waited for; matrix products, arithmetic and copies ran while one was open for 1% of the time, Pallas kernels for 0%

commit v1 on v0

v1 whole, which is shorter than its diff:
```python
import functools

import jax
import jax.numpy as jnp
from jax import lax
from jax.experimental import pallas as pl
from jax.experimental.pallas import tpu as pltpu
from jax.sharding import PartitionSpec as P

MESH = pl.DeviceIdType.MESH
XS = 4


def peer_step(i, ys):
    half = (i + 1) // 2
    return lax.rem(ys // 2 + jnp.where(i % 2 == 1, -half, half) + ys, ys)


def kernel(
    t_hbm, v_hbm, bid_hbm, home_hbm, slab_hbm, out_ref,
    t_v, v_v, send, recv, col, tiles, mine, other, core_in, mem_in, z_out, z_in,
    bid, home, slab, inv,
    in_sem, t_send_sem, t_recv_sem, core_sem, m_send_sem, m_recv_sem, z_send_sem, z_recv_sem,
):
    mems = lax.axis_size("mem")
    grps = lax.axis_size("grp")
    ys = mems // XS
    zs = grps // 2
    nob, ot = t_v.shape[0], t_v.shape[1]
    tasks = slab.shape[0]
    n = out_ref.shape[1]
    groups = zs // 4

    me = lax.axis_index("mem")
    grp = lax.axis_index("grp")
    y, x = me // XS, lax.rem(me, XS)
    z, core = grp // 2, lax.rem(grp, 2)

    def mem_peer(t):
        py = lax.rem(y + peer_step(t // XS, ys), ys)
        px = lax.rem(x + lax.rem(t, XS), XS)
        return py * XS + px

    own = mems - XS
    spans = ((0, own), (own + 1, mems))

    def over_peers(body):
        for lo, hi in spans:
            lax.fori_loop(lo, hi, lambda t, c: (body(t), c)[1], 0)

    loads = [
        pltpu.make_async_copy(src, dst, in_sem.at[i])
        for i, (src, dst) in enumerate(
            ((bid_hbm, bid), (home_hbm, home), (slab_hbm, slab), (t_hbm, t_v), (v_hbm, v_v))
        )
    ]
    for load in loads:
        load.start()

    barrier = pltpu.get_barrier_semaphore()
    over_peers(
        lambda t: pl.semaphore_signal(barrier, inc=1, device_id=(grp, mem_peer(t)), device_id_type=MESH)
    )
    sibling = z * 2 + 1 - core
    pl.semaphore_signal(barrier, inc=1, device_id=(sibling, me), device_id_type=MESH)

    def z_peer(k):
        return lax.rem(z + k, zs)

    def z_hello(k, c):
        pl.semaphore_signal(barrier, inc=1, device_id=(z_peer(k) * 2 + core, me), device_id_type=MESH)
        return c

    lax.fori_loop(1, zs, z_hello, 0)

    for load in loads[:4]:
        load.wait()

    def tile_for(p):
        q = bid[0, p]
        start = home[0, q * nob] // nob
        o = lax.rem(me - start + mems, mems)
        return lax.rem(home[0, q * nob + jnp.minimum(o, nob - 1)], nob)

    def pack(t):
        send[t] = t_v[tile_for(mem_peer(t))]

    over_peers(pack)
    recv[own] = t_v[tile_for(me)]

    pl.semaphore_wait(barrier, mems - 1 + 1 + zs - 1)

    def tile_copy(t):
        return pltpu.make_async_remote_copy(
            src_ref=send.at[t],
            dst_ref=recv.at[t],
            send_sem=t_send_sem.at[t],
            recv_sem=t_recv_sem.at[t],
            device_id=(grp, mem_peer(t)),
            device_id_type=MESH,
        )

    over_peers(lambda t: tile_copy(t).start())

    def locate(p, c):
        at = jnp.int32(tasks)
        for b in range(tasks):
            at = jnp.where(slab[b, 0, me] == p, b, at)
        inv[p] = at
        return c

    lax.fori_loop(0, mems, locate, 0)
    tiles[...] = jnp.zeros_like(tiles)
    loads[4].wait()

    over_peers(lambda t: tile_copy(t).wait_recv())

    first = home[0, bid[0, me] * nob] // nob
    for o in range(nob):
        src = lax.rem(first + o, mems)
        dy = lax.rem(y - src // XS + ys, ys)
        dx = lax.rem(x - lax.rem(src, XS) + XS, XS)
        e = dy - ys // 2
        t = jnp.where(e < 0, -2 * e - 1, 2 * e) * XS + dx
        col[o * ot:(o + 1) * ot, :] = recv[t]

    result = lax.dot_general(
        col[...], v_v[...], (((1,), (1,)), ((), ())), preferred_element_type=jnp.float32
    )

    row = lax.broadcasted_iota(jnp.int32, (8, n), 0)
    upper = lax.rem(row // 2, 2) == 1
    for b in range(tasks):
        for c in range(2):
            parts = []
            for k in range(groups):
                lo = result[k * 8:(k + 1) * 8, b * n:(b + 1) * n]
                hi = result[(k + groups) * 8:(k + groups + 1) * 8, b * n:(b + 1) * n]
                if c == 0:
                    parts.append(jnp.where(upper, pltpu.roll(hi, 2, 0), lo))
                else:
                    parts.append(jnp.where(upper, hi, pltpu.roll(lo, 6, 0)))
            tiles[c, b] = jnp.concatenate(parts, axis=1) if groups > 1 else parts[0]

    def spread(p, c):
        at = inv[p]
        other[p] = tiles[1 - core, at]
        mine[p] = tiles[core, at]
        return c

    lax.fori_loop(0, mems, spread, 0)

    to_sibling = pltpu.make_async_remote_copy(
        src_ref=other,
        dst_ref=core_in,
        send_sem=core_sem.at[0],
        recv_sem=core_sem.at[1],
        device_id=(sibling, me),
        device_id_type=MESH,
    )
    to_sibling.start()
    to_sibling.wait_recv()
    mine[...] = mine[...] + core_in[...]

    def slab_copy(t):
        p = mem_peer(t)
        return pltpu.make_async_remote_copy(
            src_ref=mine.at[p],
            dst_ref=mem_in.at[t],
            send_sem=m_send_sem.at[t],
            recv_sem=m_recv_sem.at[t],
            device_id=(grp, p),
            device_id_type=MESH,
        )

    over_peers(lambda t: slab_copy(t).start())
    mem_in[own] = mine[me]
    over_peers(lambda t: slab_copy(t).wait_recv())
    total = jnp.sum(mem_in[...], axis=0)
    for r in range(4):
        z_out[r] = total[2 * r:2 * r + 2, :]

    def rows_of(o):
        return lax.rem(o, 2) * 2 + jnp.where(o // 2 >= groups, 1, 0)

    def z_copy(k):
        to = z_peer(k)
        return pltpu.make_async_remote_copy(
            src_ref=z_out.at[rows_of(to)],
            dst_ref=z_in.at[k],
            send_sem=z_send_sem.at[k],
            recv_sem=z_recv_sem.at[k],
            device_id=(to * 2 + core, me),
            device_id_type=MESH,
        )

    lax.fori_loop(1, zs, lambda k, c: (z_copy(k).start(), c)[1], 0)
    z_in[0] = z_out[rows_of(z)]
    lax.fori_loop(1, zs, lambda k, c: (z_copy(k).wait_recv(), c)[1], 0)
    owned = jnp.sum(z_in[...], axis=0)
    group = lax.rem(z // 2, groups)
    out = owned[:, 0:n]
    for k in range(1, groups):
        out = jnp.where(group == k, owned[:, k * n:(k + 1) * n], out)
    out_ref[...] = out

    over_peers(lambda t: tile_copy(t).wait_send())
    to_sibling.wait_send()
    over_peers(lambda t: slab_copy(t).wait_send())
    lax.fori_loop(1, zs, lambda k, c: (z_copy(k).wait_send(), c)[1], 0)


def body(t_store, v_blocks, block_id, tile_home, task_slab):
    mems = lax.axis_size("mem")
    zs = lax.axis_size("grp") // 2
    nob, ot, width = t_store.shape
    tasks, n, _ = v_blocks.shape
    lanes = zs // 4 * n
    any_ref = pl.BlockSpec(memory_space=pl.ANY)
    dma = pltpu.SemaphoreType.DMA
    return pl.pallas_call(
        kernel,
        out_shape=jax.ShapeDtypeStruct((2, n), jnp.float32),
        in_specs=[any_ref] * 5,
        out_specs=pl.BlockSpec(memory_space=pltpu.VMEM),
        scratch_shapes=[
            pltpu.VMEM((nob, ot, width), jnp.bfloat16),
            pltpu.VMEM((tasks * n, width), jnp.bfloat16),
            pltpu.VMEM((mems, ot, width), jnp.bfloat16),
            pltpu.VMEM((mems, ot, width), jnp.bfloat16),
            pltpu.VMEM((nob * ot, width), jnp.bfloat16),
            pltpu.VMEM((2, tasks + 1, 8, lanes), jnp.float32),
            pltpu.VMEM((mems, 8, lanes), jnp.float32),
            pltpu.VMEM((mems, 8, lanes), jnp.float32),
            pltpu.VMEM((mems, 8, lanes), jnp.float32),
            pltpu.VMEM((mems, 8, lanes), jnp.float32),
            pltpu.VMEM((4, 2, lanes), jnp.float32),
            pltpu.VMEM((zs, 2, lanes), jnp.float32),
            pltpu.SMEM(block_id.shape, jnp.int32),
            pltpu.SMEM(tile_home.shape, jnp.int32),
            pltpu.SMEM((tasks, 1, mems), jnp.int32),
            pltpu.SMEM((mems,), jnp.int32),
            dma((5,)),
            dma((mems,)),
            dma((mems,)),
            dma((2,)),
            dma((mems,)),
            dma((mems,)),
            dma((zs,)),
            dma((zs,)),
        ],
        compiler_params=pltpu.CompilerParams(
            collective_id=0, has_side_effects=True, vmem_limit_bytes=60 * 1024 * 1024
        ),
        name="ladder",
    )(t_store, v_blocks.reshape(tasks * n, width), block_id, tile_home, jnp.transpose(task_slab, (2, 0, 1)))


def solution(mesh):
    return jax.shard_map(
        body,
        mesh=mesh,
        in_specs=(
            P(("grp", "mem"), None, None),
            P(("grp", "mem"), None, None),
            P("grp", None),
            P("grp", None),
            P("grp", None, None),
        ),
        out_specs=P("grp", "mem"),
        check_vma=False,
    )
```

time: 198 us -> 70.6 us (0.36)
  blocking collectives: 111 us -> 0 us
  Pallas kernels: 0 us -> 69.2 us
  local copies, waits for them, and re-layouts: 29.3 us -> 1.24 us
  waiting for transfers between devices: 26.6 us -> 0 us
  starting transfers between devices: 17.4 us -> 0 us
  other arithmetic: 9.14 us -> 0 us
  matrix products: 2.49 us -> 0 us
    unnamed x1 -> x0, blocking collectives: 111 us -> none
    pallas_call x0 -> x1, Pallas kernels: none -> 69.2 us  [body(): pl.pallas_call(kernel, out_shape=jax.ShapeDtypeStruct((2, n), jnp.float32...]
    all_to_all x2 -> x0, waiting for transfers between devices: 26.6 us -> none  [the longest x1 18.2 us: body(): lax.all_to_all(outgoing, 'mem', split_axis=0, concat_axis=0, tiled=True)]
    all_to_all x2 -> x0, starting transfers between devices: 17.4 us -> none  [the longest x1 10.6 us: body(): lax.all_to_all(outgoing, 'mem', split_axis=0, concat_axis=0, tiled=True)]
    unnamed x14 -> x1, local copies, waits for them, and re-layouts: 17.5 us -> 1.24 us
    gather x6 -> x0, local copies, waits for them, and re-layouts: 9.78 us -> none  [the longest x2 3.89 us: body(): fetched = jnp.take(flat_in, row_index, axis=0).reshape(occ_rows, pair_width)]
    select_n x6 -> x0, other arithmetic: 5.89 us -> none  [the longest x2 5.79 us: pack_tiles(): jnp.where(filled[:, :, None], picked, jnp.zeros((), flat_store.dtype))]
    dot_general x2 -> x0, matrix products: 2.49 us -> none  [the longest x1 2 us: body(): jnp.einsum('rk,bnk->rbn', fetched, v_blocks, preferred_element_type=jnp.f...]
  transfers between devices with their start and end apart: 2 -> 0, of which waited for: 2 -> 0; matrix products, arithmetic and copies ran while one was open for 1% -> 0% of each run, Pallas kernels for 0% -> 0%
where the time goes in v1:
time: 70.6 us; the launch traced here: 70.5 us
  Pallas kernels  69.2 us (98%)
  local copies, waits for them, and re-layouts  1.24 us (2%)
    pallas_call x1, Pallas kernels, body(): pl.pallas_call(kernel, out_shape=jax.ShapeDtypeStruct((2, n), jnp.float32...  69.2 us

profile of v1, /device:TPU:1, one launch (start us, length us, event | category | flops | bytes accessed | tf_op | source)
XLA Modules:
  0.0 70.5 jit_solution(9969998879572023430)
XLA Ops:
  0.0 69.2 %ladder.1 = f32[2,32]{1,0:T(2,128)} custom-call(bf16[16,4,4096]{2,1,0:T(4,128)(2,1)} %t_hbm.1, bf16[352,4096]{1,0:T(8,128)(2,1)} %bitcast.2, s32[1,32]{1,0:T(1,128)} %bid_hbm.1, s32[1,512]{1,0:T(1,128)} %home_hbm.1, s32[11,1,32]{2,1,0:T(1,128)} %bitcast.3), custom_call_target="tpu_custom_call" | custom-call | tf_op jit(solution)/shard_map/ladder/pallas_call | solution.py:221
  69.2 1.2 %copy.7 = f32[2,32]{1,0:T(2,128)} copy(f32[2,32]{1,0:T(2,128)} %ladder.1) | data formatting | bytes 512

commit v2 on v1

--- a/solution.py
+++ b/solution.py
@@ -11,16 +11,24 @@
 XS = 4
 
 
-def peer_step(i, ys):
-    half = (i + 1) // 2
-    return lax.rem(ys // 2 + jnp.where(i % 2 == 1, -half, half) + ys, ys)
+def offset(t, ys):
+    g, s = t // (2 * XS), lax.rem(t, 2)
+    dy = jnp.where(s == 0, ys // 2 - g, jnp.where(g == 0, 0, ys // 2 + g))
+    return dy, lax.rem(t // 2, XS)
+
+
+def step_of(dy, dx, ys):
+    g = jnp.where(dy == 0, 0, jnp.where(dy <= ys // 2, ys // 2 - dy, dy - ys // 2))
+    s = jnp.where((dy == 0) | (dy > ys // 2), 1, 0)
+    return g * 2 * XS + dx * 2 + s
 
 
 def kernel(
     t_hbm, v_hbm, bid_hbm, home_hbm, slab_hbm, out_ref,
-    t_v, v_v, send, recv, col, tiles, mine, other, core_in, mem_in, z_out, z_in,
+    t_v, v_v, send, recv, col, tiles, mine, other, core_in, m_in, z_out, z_in,
     bid, home, slab, inv,
-    in_sem, t_send_sem, t_recv_sem, core_sem, m_send_sem, m_recv_sem, z_send_sem, z_recv_sem,
+    in_sem, t_send_sem, t_recv_sem, c_send_sem, c_recv_sem, m_send_sem, m_recv_sem,
+    z_send_sem, z_recv_sem, up_sem, down_sem,
 ):
     mems = lax.axis_size("mem")
     grps = lax.axis_size("grp")
@@ -37,15 +45,13 @@
     z, core = grp // 2, lax.rem(grp, 2)
 
     def mem_peer(t):
-        py = lax.rem(y + peer_step(t // XS, ys), ys)
-        px = lax.rem(x + lax.rem(t, XS), XS)
-        return py * XS + px
-
-    own = mems - XS
-    spans = ((0, own), (own + 1, mems))
+        dy, dx = offset(t, ys)
+        return lax.rem(y + dy, ys) * XS + lax.rem(x + dx, XS)
+
+    own = 1
 
     def over_peers(body):
-        for lo, hi in spans:
+        for lo, hi in ((0, own), (own + 1, mems)):
             lax.fori_loop(lo, hi, lambda t, c: (body(t), c)[1], 0)
 
     loads = [
@@ -64,14 +70,16 @@
     sibling = z * 2 + 1 - core
     pl.semaphore_signal(barrier, inc=1, device_id=(sibling, me), device_id_type=MESH)
 
-    def z_peer(k):
-        return lax.rem(z + k, zs)
-
-    def z_hello(k, c):
-        pl.semaphore_signal(barrier, inc=1, device_id=(z_peer(k) * 2 + core, me), device_id_type=MESH)
-        return c
-
-    lax.fori_loop(1, zs, z_hello, 0)
+    def tell(to, semaphore):
+        pl.semaphore_signal(semaphore, inc=1, device_id=(to * 2 + core, me), device_id_type=MESH)
+
+    @pl.when(z > 0)
+    def _():
+        tell(z - 1, barrier)
+
+    @pl.when(z < zs - 1)
+    def _():
+        tell(z + 1, barrier)
 
     for load in loads[:4]:
         load.wait()
@@ -88,7 +96,7 @@
     over_peers(pack)
     recv[own] = t_v[tile_for(me)]
 
-    pl.semaphore_wait(barrier, mems - 1 + 1 + zs - 1)
+    pl.semaphore_wait(barrier, mems + jnp.where(z > 0, 1, 0) + jnp.where(z < zs - 1, 1, 0))
 
     def tile_copy(t):
         return pltpu.make_async_remote_copy(
@@ -102,6 +110,19 @@
 
     over_peers(lambda t: tile_copy(t).start())
 
+    @pl.when(z > 0)
+    def _():
+        pl.semaphore_wait(up_sem, 1)
+
+    @pl.when(z < zs - 1)
+    def _():
+        tell(z + 1, up_sem)
+        pl.semaphore_wait(down_sem, 1)
+
+    @pl.when(z > 0)
+    def _():
+        tell(z - 1, down_sem)
+
     def locate(p, c):
         at = jnp.int32(tasks)
         for b in range(tasks):
@@ -120,8 +141,7 @@
         src = lax.rem(first + o, mems)
         dy = lax.rem(y - src // XS + ys, ys)
         dx = lax.rem(x - lax.rem(src, XS) + XS, XS)
-        e = dy - ys // 2
-        t = jnp.where(e < 0, -2 * e - 1, 2 * e) * XS + dx
+        t = step_of(dy, dx, ys)
         col[o * ot:(o + 1) * ot, :] = recv[t]
 
     result = lax.dot_general(
@@ -142,41 +162,54 @@
                     parts.append(jnp.where(upper, hi, pltpu.roll(lo, 6, 0)))
             tiles[c, b] = jnp.concatenate(parts, axis=1) if groups > 1 else parts[0]
 
-    def spread(p, c):
-        at = inv[p]
-        other[p] = tiles[1 - core, at]
-        mine[p] = tiles[core, at]
-        return c
-
-    lax.fori_loop(0, mems, spread, 0)
-
-    to_sibling = pltpu.make_async_remote_copy(
-        src_ref=other,
-        dst_ref=core_in,
-        send_sem=core_sem.at[0],
-        recv_sem=core_sem.at[1],
-        device_id=(sibling, me),
-        device_id_type=MESH,
-    )
-    to_sibling.start()
-    to_sibling.wait_recv()
-    mine[...] = mine[...] + core_in[...]
-
-    def slab_copy(t):
-        p = mem_peer(t)
+    def core_copy(dx):
+        to = lax.rem(x + dx, XS)
         return pltpu.make_async_remote_copy(
-            src_ref=mine.at[p],
-            dst_ref=mem_in.at[t],
-            send_sem=m_send_sem.at[t],
-            recv_sem=m_recv_sem.at[t],
-            device_id=(grp, p),
+            src_ref=other.at[to],
+            dst_ref=core_in.at[to],
+            send_sem=c_send_sem.at[dx],
+            recv_sem=c_recv_sem.at[dx],
+            device_id=(sibling, me),
             device_id_type=MESH,
         )
 
-    over_peers(lambda t: slab_copy(t).start())
-    mem_in[own] = mine[me]
-    over_peers(lambda t: slab_copy(t).wait_recv())
-    total = jnp.sum(mem_in[...], axis=0)
+    x_order = (2, 1, 3, 0)
+    y_all = sorted(range(ys), key=lambda dy: -min(dy, ys - dy))
+
+    def m_copy(dx, dy):
+        tx = lax.rem(x + dx, XS)
+        ty = lax.rem(y + dy, ys)
+        return pltpu.make_async_remote_copy(
+            src_ref=mine.at[tx, ty],
+            dst_ref=m_in.at[dx, dy],
+            send_sem=m_send_sem.at[dx * ys + dy],
+            recv_sem=m_recv_sem.at[dx * ys + dy],
+            device_id=(grp, ty * XS + tx),
+            device_id_type=MESH,
+        )
+
+    for dx in x_order:
+        to = lax.rem(x + dx, XS)
+        for r in range(ys):
+            other[to, r] = tiles[1 - core, inv[r * XS + to]]
+        core_copy(dx).start()
+    for dx in x_order:
+        to = lax.rem(x + dx, XS)
+        for r in range(ys):
+            mine[to, r] = tiles[core, inv[r * XS + to]]
+    for dx in x_order:
+        to = lax.rem(x + dx, XS)
+        core_copy(dx).wait_recv()
+        mine[to] = mine[to] + core_in[to]
+        for dy in y_all:
+            if dx or dy:
+                m_copy(dx, dy).start()
+    total = mine[x, y]
+    for dx in x_order:
+        for dy in y_all:
+            if dx or dy:
+                m_copy(dx, dy).wait_recv()
+                total = total + m_in[dx, dy]
     for r in range(4):
         z_out[r] = total[2 * r:2 * r + 2, :]
 
@@ -184,7 +217,7 @@
         return lax.rem(o, 2) * 2 + jnp.where(o // 2 >= groups, 1, 0)
 
     def z_copy(k):
-        to = z_peer(k)
+        to = lax.rem(z + k, zs)
         return pltpu.make_async_remote_copy(
             src_ref=z_out.at[rows_of(to)],
             dst_ref=z_in.at[k],
@@ -205,13 +238,17 @@
     out_ref[...] = out
 
     over_peers(lambda t: tile_copy(t).wait_send())
-    to_sibling.wait_send()
-    over_peers(lambda t: slab_copy(t).wait_send())
+    for dx in x_order:
+        core_copy(dx).wait_send()
+        for dy in y_all:
+            if dx or dy:
+                m_copy(dx, dy).wait_send()
     lax.fori_loop(1, zs, lambda k, c: (z_copy(k).wait_send(), c)[1], 0)
 
 
 def body(t_store, v_blocks, block_id, tile_home, task_slab):
     mems = lax.axis_size("mem")
+    ys = mems // XS
     zs = lax.axis_size("grp") // 2
     nob, ot, width = t_store.shape
     tasks, n, _ = v_blocks.shape
@@ -230,10 +267,10 @@
             pltpu.VMEM((mems, ot, width), jnp.bfloat16),
             pltpu.VMEM((nob * ot, width), jnp.bfloat16),
             pltpu.VMEM((2, tasks + 1, 8, lanes), jnp.float32),
-            pltpu.VMEM((mems, 8, lanes), jnp.float32),
-            pltpu.VMEM((mems, 8, lanes), jnp.float32),
-            pltpu.VMEM((mems, 8, lanes), jnp.float32),
-            pltpu.VMEM((mems, 8, lanes), jnp.float32),
+            pltpu.VMEM((XS, ys, 8, lanes), jnp.float32),
+            pltpu.VMEM((XS, ys, 8, lanes), jnp.float32),
+            pltpu.VMEM((XS, ys, 8, lanes), jnp.float32),
+            pltpu.VMEM((XS, ys, 8, lanes), jnp.float32),
             pltpu.VMEM((4, 2, lanes), jnp.float32),
             pltpu.VMEM((zs, 2, lanes), jnp.float32),
             pltpu.SMEM(block_id.shape, jnp.int32),
@@ -243,11 +280,14 @@
             dma((5,)),
             dma((mems,)),
             dma((mems,)),
-            dma((2,)),
+            dma((XS,)),
+            dma((XS,)),
             dma((mems,)),
             dma((mems,)),
             dma((zs,)),
             dma((zs,)),
+            pltpu.SemaphoreType.REGULAR,
+            pltpu.SemaphoreType.REGULAR,
         ],
         compiler_params=pltpu.CompilerParams(
             collective_id=0, has_side_effects=True, vmem_limit_bytes=60 * 1024 * 1024

time: 70.6 us -> 66.4 us (0.941)
  Pallas kernels: 69.2 us -> 65 us
    pallas_call x1, Pallas kernels: 69.2 us -> 65 us  [body(): pl.pallas_call(kernel, out_shape=jax.ShapeDtypeStruct((2, n), jnp.float32...]
where the time goes in v2:
time: 66.4 us; the launch traced here: 66.3 us
  Pallas kernels  65 us (98%)
  local copies, waits for them, and re-layouts  1.24 us (2%)
    pallas_call x1, Pallas kernels, body(): pl.pallas_call(kernel, out_shape=jax.ShapeDtypeStruct((2, n), jnp.float32...  65 us

profile of v2, /device:TPU:1, one launch (start us, length us, event | category | flops | bytes accessed | tf_op | source)
XLA Modules:
  0.0 66.3 jit_solution(5301638358441051555)
XLA Ops:
  0.0 65.0 %ladder.1 = f32[2,32]{1,0:T(2,128)} custom-call(bf16[16,4,4096]{2,1,0:T(4,128)(2,1)} %t_hbm.1, bf16[352,4096]{1,0:T(8,128)(2,1)} %bitcast.2, s32[1,32]{1,0:T(1,128)} %bid_hbm.1, s32[1,512]{1,0:T(1,128)} %home_hbm.1, s32[11,1,32]{2,1,0:T(1,128)} %bitcast.3), custom_call_target="tpu_custom_call" | custom-call | tf_op jit(solution)/shard_map/ladder/pallas_call | solution.py:258
  65.0 1.2 %copy.7 = f32[2,32]{1,0:T(2,128)} copy(f32[2,32]{1,0:T(2,128)} %ladder.1) | data formatting | bytes 512

commit v3 on v2

--- a/solution.py
+++ b/solution.py
@@ -11,16 +11,8 @@
 XS = 4
 
 
-def offset(t, ys):
-    g, s = t // (2 * XS), lax.rem(t, 2)
-    dy = jnp.where(s == 0, ys // 2 - g, jnp.where(g == 0, 0, ys // 2 + g))
-    return dy, lax.rem(t // 2, XS)
-
-
-def step_of(dy, dx, ys):
-    g = jnp.where(dy == 0, 0, jnp.where(dy <= ys // 2, ys // 2 - dy, dy - ys // 2))
-    s = jnp.where((dy == 0) | (dy > ys // 2), 1, 0)
-    return g * 2 * XS + dx * 2 + s
+def farthest_first(size):
+    return sorted(range(size), key=lambda d: -min(d, size - d))
 
 
 def kernel(
@@ -28,7 +20,7 @@
     t_v, v_v, send, recv, col, tiles, mine, other, core_in, m_in, z_out, z_in,
     bid, home, slab, inv,
     in_sem, t_send_sem, t_recv_sem, c_send_sem, c_recv_sem, m_send_sem, m_recv_sem,
-    z_send_sem, z_recv_sem, up_sem, down_sem,
+    z_send_sem, z_recv_sem, near_sem, above_sem, up_sem, all_sem,
 ):
     mems = lax.axis_size("mem")
     grps = lax.axis_size("grp")
@@ -44,45 +36,41 @@
     y, x = me // XS, lax.rem(me, XS)
     z, core = grp // 2, lax.rem(grp, 2)
 
-    def mem_peer(t):
-        dy, dx = offset(t, ys)
-        return lax.rem(y + dy, ys) * XS + lax.rem(x + dx, XS)
-
-    own = 1
-
-    def over_peers(body):
-        for lo, hi in ((0, own), (own + 1, mems)):
-            lax.fori_loop(lo, hi, lambda t, c: (body(t), c)[1], 0)
+    at_y = [lax.rem(y + dy, ys) for dy in range(ys)]
+    at_x = [lax.rem(x + dx, XS) for dx in range(XS)]
+    x_order = farthest_first(XS)
+    y_order = farthest_first(ys)
+
+    def mem_peer(dy, dx):
+        return at_y[dy] * XS + at_x[dx]
+
+    barrier = pltpu.get_barrier_semaphore()
+    near = [(dy, dx) for dx in x_order for dy in (1, ys - 1, 0) if dy or dx]
+    for dy, dx in near:
+        pl.semaphore_signal(barrier, inc=1, device_id=(grp, mem_peer(dy, dx)), device_id_type=MESH)
+    sibling = z * 2 + 1 - core
+    pl.semaphore_signal(barrier, inc=1, device_id=(sibling, me), device_id_type=MESH)
+
+    def tell(to, semaphore):
+        pl.semaphore_signal(semaphore, inc=1, device_id=(to * 2 + core, me), device_id_type=MESH)
+
+    @pl.when(z < zs - 1)
+    def _():
+        tell(z + 1, barrier)
 
     loads = [
         pltpu.make_async_copy(src, dst, in_sem.at[i])
         for i, (src, dst) in enumerate(
-            ((bid_hbm, bid), (home_hbm, home), (slab_hbm, slab), (t_hbm, t_v), (v_hbm, v_v))
+            ((t_hbm, t_v), (home_hbm, home), (bid_hbm, bid), (slab_hbm, slab), (v_hbm, v_v))
         )
     ]
-    for load in loads:
+    for load in loads[:3]:
         load.start()
 
-    barrier = pltpu.get_barrier_semaphore()
-    over_peers(
-        lambda t: pl.semaphore_signal(barrier, inc=1, device_id=(grp, mem_peer(t)), device_id_type=MESH)
-    )
-    sibling = z * 2 + 1 - core
-    pl.semaphore_signal(barrier, inc=1, device_id=(sibling, me), device_id_type=MESH)
-
-    def tell(to, semaphore):
-        pl.semaphore_signal(semaphore, inc=1, device_id=(to * 2 + core, me), device_id_type=MESH)
-
-    @pl.when(z > 0)
-    def _():
-        tell(z - 1, barrier)
-
-    @pl.when(z < zs - 1)
-    def _():
-        tell(z + 1, barrier)
-
-    for load in loads[:4]:
+    for load in loads[:3]:
         load.wait()
+    for load in loads[3:]:
+        load.start()
 
     def tile_for(p):
         q = bid[0, p]
@@ -90,38 +78,63 @@
         o = lax.rem(me - start + mems, mems)
         return lax.rem(home[0, q * nob + jnp.minimum(o, nob - 1)], nob)
 
-    def pack(t):
-        send[t] = t_v[tile_for(mem_peer(t))]
-
-    over_peers(pack)
-    recv[own] = t_v[tile_for(me)]
-
-    pl.semaphore_wait(barrier, mems + jnp.where(z > 0, 1, 0) + jnp.where(z < zs - 1, 1, 0))
-
-    def tile_copy(t):
-        return pltpu.make_async_remote_copy(
-            src_ref=send.at[t],
-            dst_ref=recv.at[t],
-            send_sem=t_send_sem.at[t],
-            recv_sem=t_recv_sem.at[t],
-            device_id=(grp, mem_peer(t)),
-            device_id_type=MESH,
-        )
-
-    over_peers(lambda t: tile_copy(t).start())
+    def tile_copy(dy, dx):
+        slot = dy * XS + dx
+        return pltpu.make_async_remote_copy(
+            src_ref=send.at[slot],
+            dst_ref=recv.at[slot],
+            send_sem=t_send_sem.at[slot],
+            recv_sem=t_recv_sem.at[slot],
+            device_id=(grp, mem_peer(dy, dx)),
+            device_id_type=MESH,
+        )
+
+    pl.semaphore_wait(barrier, len(near) + 1 + jnp.where(z > 0, 1, 0))
 
     @pl.when(z > 0)
     def _():
+        tell(z - 1, above_sem)
+
+    def tell_rows(d):
+        for dy in (1, ys - 1):
+            pl.semaphore_signal(near_sem.at[d], inc=1, device_id=(grp, mem_peer(dy, 0)), device_id_type=MESH)
+
+    tell_rows(1)
+    half = ys // 2
+    last = sorted({half, half - 1, ys - half + 1} - {1, ys - 1}, key=lambda d: -min(d, ys - d))
+    plan = [near]
+    plan += [[(dy, dx) for dx in x_order for dy in (d, ys - d)] for d in range(2, half - 1)]
+    plan += [[(dy, dx) for dx in x_order for dy in last]]
+    sent = []
+    known = 1
+    for rows in plan:
+        for d in range(known + 1, max(min(dy, ys - dy) for dy, _ in rows) + 1):
+            pl.semaphore_wait(near_sem.at[d - 1], 2)
+            if d < half:
+                tell_rows(d)
+            known = d
+        for dy, dx in rows:
+            send[dy * XS + dx] = t_v[tile_for(mem_peer(dy, dx))]
+            tile_copy(dy, dx).start()
+        sent += rows
+    recv[0] = t_v[tile_for(me)]
+
+    @pl.when(z < zs - 1)
+    def _():
+        pl.semaphore_wait(above_sem, 1)
+
+    @pl.when(z > 0)
+    def _():
         pl.semaphore_wait(up_sem, 1)
 
     @pl.when(z < zs - 1)
     def _():
         tell(z + 1, up_sem)
-        pl.semaphore_wait(down_sem, 1)
-
-    @pl.when(z > 0)
-    def _():
-        tell(z - 1, down_sem)
+
+    @pl.when(z == zs - 1)
+    def _():
+        for to in range(zs - 1):
+            tell(to, all_sem)
 
     def locate(p, c):
         at = jnp.int32(tasks)
@@ -130,18 +143,24 @@
         inv[p] = at
         return c
 
+    loads[3].wait()
     lax.fori_loop(0, mems, locate, 0)
     tiles[...] = jnp.zeros_like(tiles)
     loads[4].wait()
 
-    over_peers(lambda t: tile_copy(t).wait_recv())
+    @pl.when(z < zs - 1)
+    def _():
+        pl.semaphore_wait(all_sem, 1)
+
+    for dy, dx in sent:
+        tile_copy(dy, dx).wait_recv()
 
     first = home[0, bid[0, me] * nob] // nob
     for o in range(nob):
         src = lax.rem(first + o, mems)
         dy = lax.rem(y - src // XS + ys, ys)
         dx = lax.rem(x - lax.rem(src, XS) + XS, XS)
-        t = step_of(dy, dx, ys)
+        t = dy * XS + dx
         col[o * ot:(o + 1) * ot, :] = recv[t]
 
     result = lax.dot_general(
@@ -163,7 +182,7 @@
             tiles[c, b] = jnp.concatenate(parts, axis=1) if groups > 1 else parts[0]
 
     def core_copy(dx):
-        to = lax.rem(x + dx, XS)
+        to = at_x[dx]
         return pltpu.make_async_remote_copy(
             src_ref=other.at[to],
             dst_ref=core_in.at[to],
@@ -173,12 +192,8 @@
             device_id_type=MESH,
         )
 
-    x_order = (2, 1, 3, 0)
-    y_all = sorted(range(ys), key=lambda dy: -min(dy, ys - dy))
-
     def m_copy(dx, dy):
-        tx = lax.rem(x + dx, XS)
-        ty = lax.rem(y + dy, ys)
+        tx, ty = at_x[dx], at_y[dy]
         return pltpu.make_async_remote_copy(
             src_ref=mine.at[tx, ty],
             dst_ref=m_in.at[dx, dy],
@@ -189,24 +204,24 @@
         )
 
     for dx in x_order:
-        to = lax.rem(x + dx, XS)
+        to = at_x[dx]
         for r in range(ys):
             other[to, r] = tiles[1 - core, inv[r * XS + to]]
         core_copy(dx).start()
     for dx in x_order:
-        to = lax.rem(x + dx, XS)
+        to = at_x[dx]
         for r in range(ys):
             mine[to, r] = tiles[core, inv[r * XS + to]]
     for dx in x_order:
-        to = lax.rem(x + dx, XS)
+        to = at_x[dx]
         core_copy(dx).wait_recv()
         mine[to] = mine[to] + core_in[to]
-        for dy in y_all:
+        for dy in y_order:
             if dx or dy:
                 m_copy(dx, dy).start()
     total = mine[x, y]
     for dx in x_order:
-        for dy in y_all:
+        for dy in y_order:
             if dx or dy:
                 m_copy(dx, dy).wait_recv()
                 total = total + m_in[dx, dy]
@@ -216,34 +231,52 @@
     def rows_of(o):
         return lax.rem(o, 2) * 2 + jnp.where(o // 2 >= groups, 1, 0)
 
-    def z_copy(k):
-        to = lax.rem(z + k, zs)
+    def other_plane(i):
+        return i - jnp.where(i > z, 0, 1)
+
+    def z_copy(i):
+        to = other_plane(i)
         return pltpu.make_async_remote_copy(
             src_ref=z_out.at[rows_of(to)],
-            dst_ref=z_in.at[k],
-            send_sem=z_send_sem.at[k],
-            recv_sem=z_recv_sem.at[k],
+            dst_ref=z_in.at[z],
+            send_sem=z_send_sem.at[to],
+            recv_sem=z_recv_sem.at[z],
             device_id=(to * 2 + core, me),
             device_id_type=MESH,
         )
 
-    lax.fori_loop(1, zs, lambda k, c: (z_copy(k).start(), c)[1], 0)
-    z_in[0] = z_out[rows_of(z)]
-    lax.fori_loop(1, zs, lambda k, c: (z_copy(k).wait_recv(), c)[1], 0)
-    owned = jnp.sum(z_in[...], axis=0)
+    def z_arrival(i):
+        src = other_plane(i)
+        return pltpu.make_async_remote_copy(
+            src_ref=z_out.at[0],
+            dst_ref=z_in.at[src],
+            send_sem=z_send_sem.at[src],
+            recv_sem=z_recv_sem.at[src],
+            device_id=(src * 2 + core, me),
+            device_id_type=MESH,
+        )
+
+    for i in range(1, zs):
+        z_copy(i).start()
+    owned = z_out[rows_of(z)]
+    for i in range(1, zs):
+        z_arrival(i).wait_recv()
+        owned = owned + z_in[other_plane(i)]
     group = lax.rem(z // 2, groups)
     out = owned[:, 0:n]
     for k in range(1, groups):
         out = jnp.where(group == k, owned[:, k * n:(k + 1) * n], out)
     out_ref[...] = out
 
-    over_peers(lambda t: tile_copy(t).wait_send())
+    for dy, dx in sent:
+        tile_copy(dy, dx).wait_send()
     for dx in x_order:
         core_copy(dx).wait_send()
-        for dy in y_all:
+        for dy in y_order:
             if dx or dy:
                 m_copy(dx, dy).wait_send()
-    lax.fori_loop(1, zs, lambda k, c: (z_copy(k).wait_send(), c)[1], 0)
+    for i in range(1, zs):
+        z_copy(i).wait_send()
 
 
 def body(t_store, v_blocks, block_id, tile_home, task_slab):
@@ -286,6 +319,8 @@
             dma((mems,)),
             dma((zs,)),
             dma((zs,)),
+            pltpu.SemaphoreType.REGULAR((ys // 2,)),
+            pltpu.SemaphoreType.REGULAR,
             pltpu.SemaphoreType.REGULAR,
             pltpu.SemaphoreType.REGULAR,
         ],

time: 66.4 us -> 64.6 us (0.973)
  Pallas kernels: 65 us -> 63.2 us
    pallas_call x1, Pallas kernels: 65 us -> 63.2 us  [body(): pl.pallas_call(kernel, out_shape=jax.ShapeDtypeStruct((2, n), jnp.float32...]
where the time goes in v3:
time: 64.6 us; the launch traced here: 64.4 us
  Pallas kernels  63.2 us (98%)
  local copies, waits for them, and re-layouts  1.24 us (2%)
    pallas_call x1, Pallas kernels, body(): pl.pallas_call(kernel, out_shape=jax.ShapeDtypeStruct((2, n), jnp.float32...  63.2 us

profile of v3, /device:TPU:1, one launch (start us, length us, event | category | flops | bytes accessed | tf_op | source)
XLA Modules:
  0.0 64.4 jit_solution(1647972828430714539)
XLA Ops:
  0.0 63.2 %ladder.1 = f32[2,32]{1,0:T(2,128)} custom-call(bf16[16,4,4096]{2,1,0:T(4,128)(2,1)} %t_hbm.1, bf16[352,4096]{1,0:T(8,128)(2,1)} %bitcast.2, s32[1,32]{1,0:T(1,128)} %bid_hbm.1, s32[1,512]{1,0:T(1,128)} %home_hbm.1, s32[11,1,32]{2,1,0:T(1,128)} %bitcast.3), custom_call_target="tpu_custom_call" | custom-call | tf_op jit(solution)/shard_map/ladder/pallas_call | solution.py:291
  63.2 1.2 %copy.7 = f32[2,32]{1,0:T(2,128)} copy(f32[2,32]{1,0:T(2,128)} %ladder.1) | data formatting | bytes 512

commit v4 on v3

--- a/solution.py
+++ b/solution.py
@@ -39,7 +39,6 @@
     at_y = [lax.rem(y + dy, ys) for dy in range(ys)]
     at_x = [lax.rem(x + dx, XS) for dx in range(XS)]
     x_order = farthest_first(XS)
-    y_order = farthest_first(ys)
 
     def mem_peer(dy, dx):
         return at_y[dy] * XS + at_x[dx]
@@ -181,50 +180,57 @@
                     parts.append(jnp.where(upper, hi, pltpu.roll(lo, 6, 0)))
             tiles[c, b] = jnp.concatenate(parts, axis=1) if groups > 1 else parts[0]
 
-    def core_copy(dx):
-        to = at_x[dx]
-        return pltpu.make_async_remote_copy(
-            src_ref=other.at[to],
-            dst_ref=core_in.at[to],
-            send_sem=c_send_sem.at[dx],
-            recv_sem=c_recv_sem.at[dx],
+    def core_copy(tx):
+        return pltpu.make_async_remote_copy(
+            src_ref=other.at[tx],
+            dst_ref=core_in.at[tx],
+            send_sem=c_send_sem.at[tx],
+            recv_sem=c_recv_sem.at[tx],
             device_id=(sibling, me),
             device_id_type=MESH,
         )
 
-    def m_copy(dx, dy):
-        tx, ty = at_x[dx], at_y[dy]
-        return pltpu.make_async_remote_copy(
-            src_ref=mine.at[tx, ty],
-            dst_ref=m_in.at[dx, dy],
-            send_sem=m_send_sem.at[dx * ys + dy],
-            recv_sem=m_recv_sem.at[dx * ys + dy],
-            device_id=(grp, ty * XS + tx),
-            device_id_type=MESH,
-        )
-
-    for dx in x_order:
-        to = at_x[dx]
+    def m_copy(p):
+        return pltpu.make_async_remote_copy(
+            src_ref=mine.at[p % XS, p // XS],
+            dst_ref=m_in.at[me],
+            send_sem=m_send_sem.at[p],
+            recv_sem=m_recv_sem.at[me],
+            device_id=(grp, p),
+            device_id_type=MESH,
+        )
+
+    def m_arrival(p):
+        return pltpu.make_async_remote_copy(
+            src_ref=mine.at[p % XS, p // XS],
+            dst_ref=m_in.at[p],
+            send_sem=m_send_sem.at[p],
+            recv_sem=m_recv_sem.at[p],
+            device_id=(grp, p),
+            device_id_type=MESH,
+        )
+
+    columns, lines = farthest_first(XS)[::-1], farthest_first(ys)[::-1]
+    for tx in columns:
         for r in range(ys):
-            other[to, r] = tiles[1 - core, inv[r * XS + to]]
-        core_copy(dx).start()
-    for dx in x_order:
-        to = at_x[dx]
+            other[tx, r] = tiles[1 - core, inv[r * XS + tx]]
+        core_copy(tx).start()
+    for tx in columns:
         for r in range(ys):
-            mine[to, r] = tiles[core, inv[r * XS + to]]
-    for dx in x_order:
-        to = at_x[dx]
-        core_copy(dx).wait_recv()
-        mine[to] = mine[to] + core_in[to]
-        for dy in y_order:
-            if dx or dy:
-                m_copy(dx, dy).start()
-    total = mine[x, y]
-    for dx in x_order:
-        for dy in y_order:
-            if dx or dy:
-                m_copy(dx, dy).wait_recv()
-                total = total + m_in[dx, dy]
+            mine[tx, r] = tiles[core, inv[r * XS + tx]]
+    for tx in columns:
+        core_copy(tx).wait_recv()
+        mine[tx] = mine[tx] + core_in[tx]
+        for ty in lines:
+            @pl.when(me != ty * XS + tx)
+            def _():
+                m_copy(ty * XS + tx).start()
+    m_in[me] = mine[x, y]
+    for p in range(mems):
+        @pl.when(me != p)
+        def _():
+            m_arrival(p).wait_recv()
+    total = jnp.sum(m_in[...], axis=0)
     for r in range(4):
         z_out[r] = total[2 * r:2 * r + 2, :]
 
@@ -270,11 +276,12 @@
 
     for dy, dx in sent:
         tile_copy(dy, dx).wait_send()
-    for dx in x_order:
-        core_copy(dx).wait_send()
-        for dy in y_order:
-            if dx or dy:
-                m_copy(dx, dy).wait_send()
+    for tx in columns:
+        core_copy(tx).wait_send()
+    for p in range(mems):
+        @pl.when(me != p)
+        def _():
+            m_copy(p).wait_send()
     for i in range(1, zs):
         z_copy(i).wait_send()
 
@@ -303,7 +310,7 @@
             pltpu.VMEM((XS, ys, 8, lanes), jnp.float32),
             pltpu.VMEM((XS, ys, 8, lanes), jnp.float32),
             pltpu.VMEM((XS, ys, 8, lanes), jnp.float32),
-            pltpu.VMEM((XS, ys, 8, lanes), jnp.float32),
+            pltpu.VMEM((mems, 8, lanes), jnp.float32),
             pltpu.VMEM((4, 2, lanes), jnp.float32),
             pltpu.VMEM((zs, 2, lanes), jnp.float32),
             pltpu.SMEM(block_id.shape, jnp.int32),

time: 64.6 us -> 64 us (level)
  no operation moved by 1% of the time
where the time goes in v4:
time: 64 us; the launch traced here: 63.8 us
  Pallas kernels  62.6 us (98%)
  local copies, waits for them, and re-layouts  1.24 us (2%)
    pallas_call x1, Pallas kernels, body(): pl.pallas_call(kernel, out_shape=jax.ShapeDtypeStruct((2, n), jnp.float32...  62.6 us

profile of v4, /device:TPU:1, one launch (start us, length us, event | category | flops | bytes accessed | tf_op | source)
XLA Modules:
  0.0 63.8 jit_solution(2840498051359295677)
XLA Ops:
  0.0 62.6 %ladder.1 = f32[2,32]{1,0:T(2,128)} custom-call(bf16[16,4,4096]{2,1,0:T(4,128)(2,1)} %t_hbm.1, bf16[352,4096]{1,0:T(8,128)(2,1)} %bitcast.2, s32[1,32]{1,0:T(1,128)} %bid_hbm.1, s32[1,512]{1,0:T(1,128)} %home_hbm.1, s32[11,1,32]{2,1,0:T(1,128)} %bitcast.3), custom_call_target="tpu_custom_call" | custom-call | tf_op jit(solution)/shard_map/ladder/pallas_call | solution.py:298
  62.6 1.2 %copy.7 = f32[2,32]{1,0:T(2,128)} copy(f32[2,32]{1,0:T(2,128)} %ladder.1) | data formatting | bytes 512

commit v5 on v4

--- a/solution.py
+++ b/solution.py
@@ -82,9 +82,19 @@
         return pltpu.make_async_remote_copy(
             src_ref=send.at[slot],
             dst_ref=recv.at[slot],
-            send_sem=t_send_sem.at[slot],
-            recv_sem=t_recv_sem.at[slot],
+            send_sem=t_send_sem,
+            recv_sem=t_recv_sem,
             device_id=(grp, mem_peer(dy, dx)),
+            device_id_type=MESH,
+        )
+
+    def tile_all():
+        return pltpu.make_async_remote_copy(
+            src_ref=send.at[1:],
+            dst_ref=recv.at[1:],
+            send_sem=t_send_sem,
+            recv_sem=t_recv_sem,
+            device_id=(grp, me),
             device_id_type=MESH,
         )
 
@@ -104,7 +114,6 @@
     plan = [near]
     plan += [[(dy, dx) for dx in x_order for dy in (d, ys - d)] for d in range(2, half - 1)]
     plan += [[(dy, dx) for dx in x_order for dy in last]]
-    sent = []
     known = 1
     for rows in plan:
         for d in range(known + 1, max(min(dy, ys - dy) for dy, _ in rows) + 1):
@@ -115,7 +124,6 @@
         for dy, dx in rows:
             send[dy * XS + dx] = t_v[tile_for(mem_peer(dy, dx))]
             tile_copy(dy, dx).start()
-        sent += rows
     recv[0] = t_v[tile_for(me)]
 
     @pl.when(z < zs - 1)
@@ -151,8 +159,7 @@
     def _():
         pl.semaphore_wait(all_sem, 1)
 
-    for dy, dx in sent:
-        tile_copy(dy, dx).wait_recv()
+    tile_all().wait_recv()
 
     first = home[0, bid[0, me] * nob] // nob
     for o in range(nob):
@@ -184,7 +191,7 @@
         return pltpu.make_async_remote_copy(
             src_ref=other.at[tx],
             dst_ref=core_in.at[tx],
-            send_sem=c_send_sem.at[tx],
+            send_sem=c_send_sem,
             recv_sem=c_recv_sem.at[tx],
             device_id=(sibling, me),
             device_id_type=MESH,
@@ -194,19 +201,19 @@
         return pltpu.make_async_remote_copy(
             src_ref=mine.at[p % XS, p // XS],
             dst_ref=m_in.at[me],
-            send_sem=m_send_sem.at[p],
-            recv_sem=m_recv_sem.at[me],
+            send_sem=m_send_sem,
+            recv_sem=m_recv_sem,
             device_id=(grp, p),
             device_id_type=MESH,
         )
 
-    def m_arrival(p):
-        return pltpu.make_async_remote_copy(
-            src_ref=mine.at[p % XS, p // XS],
-            dst_ref=m_in.at[p],
-            send_sem=m_send_sem.at[p],
-            recv_sem=m_recv_sem.at[p],
-            device_id=(grp, p),
+    def m_all():
+        return pltpu.make_async_remote_copy(
+            src_ref=m_in.at[1:],
+            dst_ref=m_in.at[1:],
+            send_sem=m_send_sem,
+            recv_sem=m_recv_sem,
+            device_id=(grp, me),
             device_id_type=MESH,
         )
 
@@ -226,10 +233,7 @@
             def _():
                 m_copy(ty * XS + tx).start()
     m_in[me] = mine[x, y]
-    for p in range(mems):
-        @pl.when(me != p)
-        def _():
-            m_arrival(p).wait_recv()
+    m_all().wait_recv()
     total = jnp.sum(m_in[...], axis=0)
     for r in range(4):
         z_out[r] = total[2 * r:2 * r + 2, :]
@@ -245,45 +249,37 @@
         return pltpu.make_async_remote_copy(
             src_ref=z_out.at[rows_of(to)],
             dst_ref=z_in.at[z],
-            send_sem=z_send_sem.at[to],
-            recv_sem=z_recv_sem.at[z],
+            send_sem=z_send_sem,
+            recv_sem=z_recv_sem,
             device_id=(to * 2 + core, me),
             device_id_type=MESH,
         )
 
-    def z_arrival(i):
-        src = other_plane(i)
-        return pltpu.make_async_remote_copy(
-            src_ref=z_out.at[0],
-            dst_ref=z_in.at[src],
-            send_sem=z_send_sem.at[src],
-            recv_sem=z_recv_sem.at[src],
-            device_id=(src * 2 + core, me),
+    def z_all():
+        return pltpu.make_async_remote_copy(
+            src_ref=z_in.at[1:],
+            dst_ref=z_in.at[1:],
+            send_sem=z_send_sem,
+            recv_sem=z_recv_sem,
+            device_id=(grp, me),
             device_id_type=MESH,
         )
 
     for i in range(1, zs):
         z_copy(i).start()
-    owned = z_out[rows_of(z)]
-    for i in range(1, zs):
-        z_arrival(i).wait_recv()
-        owned = owned + z_in[other_plane(i)]
+    z_in[z] = z_out[rows_of(z)]
+    z_all().wait_recv()
+    owned = jnp.sum(z_in[...], axis=0)
     group = lax.rem(z // 2, groups)
     out = owned[:, 0:n]
     for k in range(1, groups):
         out = jnp.where(group == k, owned[:, k * n:(k + 1) * n], out)
     out_ref[...] = out
 
-    for dy, dx in sent:
-        tile_copy(dy, dx).wait_send()
-    for tx in columns:
-        core_copy(tx).wait_send()
-    for p in range(mems):
-        @pl.when(me != p)
-        def _():
-            m_copy(p).wait_send()
-    for i in range(1, zs):
-        z_copy(i).wait_send()
+    tile_all().wait_send()
+    pltpu.make_async_copy(other, core_in, c_send_sem).wait()
+    m_all().wait_send()
+    z_all().wait_send()
 
 
 def body(t_store, v_blocks, block_id, tile_home, task_slab):
@@ -318,14 +314,14 @@
             pltpu.SMEM((tasks, 1, mems), jnp.int32),
             pltpu.SMEM((mems,), jnp.int32),
             dma((5,)),
-            dma((mems,)),
-            dma((mems,)),
+            dma,
+            dma,
+            dma,
             dma((XS,)),
-            dma((XS,)),
-            dma((mems,)),
-            dma((mems,)),
-            dma((zs,)),
-            dma((zs,)),
+            dma,
+            dma,
+            dma,
+            dma,
             pltpu.SemaphoreType.REGULAR((ys // 2,)),
             pltpu.SemaphoreType.REGULAR,
             pltpu.SemaphoreType.REGULAR,

time: 64 us -> 62.5 us (0.977)
  Pallas kernels: 62.6 us -> 61.1 us
    pallas_call x1, Pallas kernels: 62.6 us -> 61.1 us  [body(): pl.pallas_call(kernel, out_shape=jax.ShapeDtypeStruct((2, n), jnp.float32...]
where the time goes in v5:
time: 62.5 us; the launch traced here: 62.3 us
  Pallas kernels  61.1 us (98%)
  local copies, waits for them, and re-layouts  1.24 us (2%)
    pallas_call x1, Pallas kernels, body(): pl.pallas_call(kernel, out_shape=jax.ShapeDtypeStruct((2, n), jnp.float32...  61.1 us

profile of v5, /device:TPU:1, one launch (start us, length us, event | category | flops | bytes accessed | tf_op | source)
XLA Modules:
  0.0 62.3 jit_solution(4510080692600293716)
XLA Ops:
  0.0 61.1 %ladder.1 = f32[2,32]{1,0:T(2,128)} custom-call(bf16[16,4,4096]{2,1,0:T(4,128)(2,1)} %t_hbm.1, bf16[352,4096]{1,0:T(8,128)(2,1)} %bitcast.2, s32[1,32]{1,0:T(1,128)} %bid_hbm.1, s32[1,512]{1,0:T(1,128)} %home_hbm.1, s32[11,1,32]{2,1,0:T(1,128)} %bitcast.3), custom_call_target="tpu_custom_call" | custom-call | tf_op jit(solution)/shard_map/ladder/pallas_call | solution.py:294
  61.1 1.2 %copy.7 = f32[2,32]{1,0:T(2,128)} copy(f32[2,32]{1,0:T(2,128)} %ladder.1) | data formatting | bytes 512

commit v6 on v5

--- a/solution.py
+++ b/solution.py
@@ -268,6 +268,9 @@
     for i in range(1, zs):
         z_copy(i).start()
     z_in[z] = z_out[rows_of(z)]
+    tile_all().wait_send()
+    pltpu.make_async_copy(other, core_in, c_send_sem).wait()
+    m_all().wait_send()
     z_all().wait_recv()
     owned = jnp.sum(z_in[...], axis=0)
     group = lax.rem(z // 2, groups)
@@ -276,9 +279,6 @@
         out = jnp.where(group == k, owned[:, k * n:(k + 1) * n], out)
     out_ref[...] = out
 
-    tile_all().wait_send()
-    pltpu.make_async_copy(other, core_in, c_send_sem).wait()
-    m_all().wait_send()
     z_all().wait_send()
 
 

time: 62.5 us -> 62.5 us (level)
  no operation moved by 1% of the time
where the time goes in v6:
time: 62.5 us; the launch traced here: 62.3 us
  Pallas kernels  61.1 us (98%)
  local copies, waits for them, and re-layouts  1.24 us (2%)
    pallas_call x1, Pallas kernels, body(): pl.pallas_call(kernel, out_shape=jax.ShapeDtypeStruct((2, n), jnp.float32...  61.1 us

profile of v6, /device:TPU:1, one launch (start us, length us, event | category | flops | bytes accessed | tf_op | source)
XLA Modules:
  0.0 62.3 jit_solution(5629886703784290523)
XLA Ops:
  0.0 61.1 %ladder.1 = f32[2,32]{1,0:T(2,128)} custom-call(bf16[16,4,4096]{2,1,0:T(4,128)(2,1)} %t_hbm.1, bf16[352,4096]{1,0:T(8,128)(2,1)} %bitcast.2, s32[1,32]{1,0:T(1,128)} %bid_hbm.1, s32[1,512]{1,0:T(1,128)} %home_hbm.1, s32[11,1,32]{2,1,0:T(1,128)} %bitcast.3), custom_call_target="tpu_custom_call" | custom-call | tf_op jit(solution)/shard_map/ladder/pallas_call | solution.py:294
  61.1 1.2 %copy.7 = f32[2,32]{1,0:T(2,128)} copy(f32[2,32]{1,0:T(2,128)} %ladder.1) | data formatting | bytes 512
